TPU v7x, 128 devices: a whole 4x4x4 slice. The times are simulated.
128 devices in a mesh: shard: 8 (over x, core), split: 16 (over z, y).
Axes of the slice: x: 4, y: 4, z: 4, core: 2. Of those that a mesh axis runs over, the one named last changes fastest.
Arguments:
- embedding: bfloat16 [65536, 512], P(('shard', 'split')), may hold values from -200 to 200
- cluster: int32 [65536], P(('shard', 'split')), may hold values from 0 to 31, as said below
- rank: int32 [65536], P(('shard', 'split')), may hold values from 0 to 1048575
Outputs:
- best_similarity: float32 [65536], P(('shard', 'split'))
Inputs may be any that keep to these rules, and one draw needn't show every extreme that they name: The rows of one device hold at most 32 rows of any one cluster, and exactly 32 rows of some cluster.
All inputs are finite; a program needn't handle non-finite values.
Results may differ from a plain program's by a relative error of at most 0.00055.
Values may be sent and summed in bfloat16 or wider, within the bound.
A program may use at most 64 MiB of HBM per device.

v0:
```python
import jax
import jax.numpy as jnp
from jax import lax
from jax.sharding import PartitionSpec as P

CL_PER = 4


rank_ceiling = 1 << 30


def masked_best(row_block, row_rank, col_block, col_rank, same_group):
    scores = lax.dot_general(
        row_block, col_block, (((1,), (1,)), ((), ())), preferred_element_type=jnp.float32
    )
    allowed = same_group & (col_rank[None, :] < row_rank[:, None])
    return jnp.max(jnp.where(allowed, scores, -1.0), axis=1)


def body(embedding, cluster, rank):
    rows_dev, width = embedding.shape
    shard_count = lax.axis_size("shard")
    cluster_count = CL_PER * shard_count
    per_cluster = 2 * rows_dev // cluster_count
    source_band = shard_count * per_cluster
    slot_count = CL_PER * source_band
    values32 = embedding.astype(jnp.float32)
    unit = (
        values32 * lax.rsqrt(jnp.sum(values32 * values32, axis=1, keepdims=True) + 1e-06)
    ).astype(jnp.bfloat16)
    target = cluster % shard_count
    column = cluster // shard_count
    onehot = (cluster[:, None] == jnp.arange(cluster_count, dtype=jnp.int32)[None, :]).astype(
        jnp.int32
    )
    position = jnp.sum((jnp.cumsum(onehot, axis=0) - onehot) * onehot, axis=1)
    slot = (column * shard_count + target) * per_cluster + position
    outgoing = jnp.zeros((slot_count, width), jnp.bfloat16).at[slot].set(unit)
    out_rank = jnp.full((slot_count,), rank_ceiling, jnp.int32).at[slot].set(rank)
    arrived, arrived_rank = (
        lax.all_to_all(
            outgoing.reshape(CL_PER, shard_count, per_cluster, width),
            "shard",
            split_axis=1,
            concat_axis=1,
            tiled=True,
        ),
        lax.all_to_all(
            out_rank.reshape(CL_PER, shard_count, per_cluster),
            "shard",
            split_axis=1,
            concat_axis=1,
            tiled=True,
        ),
    )
    row_block = arrived.reshape(slot_count, width)
    row_rank = arrived_rank.reshape(slot_count)
    start_best = jnp.full((slot_count,), -1.0, jnp.float32)
    row_group = jnp.arange(slot_count, dtype=jnp.int32) // source_band
    same_group = row_group[:, None] == row_group[None, :]
    carry = start_best
    piece_rows = lax.all_gather(row_block, "split", axis=0, tiled=True)
    piece_rank = lax.all_gather(row_rank, "split", axis=0, tiled=True)
    blocks = piece_rows.shape[0] // slot_count

    def visit(best_now, item):
        col_block, col_rank = item
        found = masked_best(row_block, row_rank, col_block, col_rank, same_group)
        return (jnp.maximum(best_now, found), None)

    carry, unused = lax.scan(
        visit,
        carry,
        (piece_rows.reshape(blocks, slot_count, width), piece_rank.reshape(blocks, slot_count)),
    )
    returned = lax.all_to_all(
        carry.reshape(CL_PER, shard_count, per_cluster),
        "shard",
        split_axis=1,
        concat_axis=1,
        tiled=True,
    )
    return returned.reshape(slot_count)[slot]


def solution(mesh):
    return jax.shard_map(
        body,
        mesh=mesh,
        in_specs=(P(("shard", "split"), None), P(("shard", "split")), P(("shard", "split"))),
        out_specs=P(("shard", "split")),
        check_vma=False,
    )
```

profile of v0, /device:TPU:1, one launch (start us, length us, event | category | flops | bytes accessed | tf_op | source)
XLA Modules:
  0.0 219.5 jit_solution(11891030443032102965)
XLA Ops:
  11.4 3.3 %scatter_custom_fusion.1 = bf16[1024,512]{1,0:T(8,128)(2,1)S(1)} fusion(s32[512]{0:T(512)S(1)} %compare_select_fusion, bf16[512,512]{1,0:T(8,128)(2,1)} %param.5, f32[512]{0:T(512)S(1)} %add_rsqrt_fusion, bf16[]{:T(256)} %constant.66.clone.1), kind=kCustom, calls=%fused_computation.16 | custom fusion | flops 786432 | bytes 1574914 | tf_op jit(solution)/shard_map/scatter | solution.py:38
  14.8 20.7 %all_to_all.15 = bf16[4,8,32,512]{3,2,0,1:T(8,128)(2,1)S(1)} all-to-all(bf16[4,8,32,512]{3,2,0,1:T(8,128)(2,1)S(1)} %copy.11), channel_id=1, replica_groups=mesh['shard'=8,'split'=16] {'shard'}, dimensions={1} | all-to-all | bytes 2097152 | tf_op jit(solution)/shard_map/all_to_all | solution.py:41
  39.9 4.2 %all-to-all-start = ((s32[8,1,128]{2,1,0:T(1,128)}), s32[8,1,128]{2,1,0:T(1,128)S(1)}, u32[]{:S(2)}, u32[]{:S(2)}) async-start(s32[8,1,128]{2,1,0:T(1,128)} %reshape.114), calls=%async_computation | async-start | bytes 8192 | tf_op jit(solution)/shard_map/all_to_all | solution.py:48
  44.1 4.6 %all-to-all-done = s32[8,1,128]{2,1,0:T(1,128)S(1)} async-done(((s32[8,1,128]{2,1,0:T(1,128)}), s32[8,1,128]{2,1,0:T(1,128)S(1)}, u32[]{:S(2)}, u32[]{:S(2)}) %all-to-all-start) | async-done | bytes 4128 | tf_op jit(solution)/shard_map/all_to_all | solution.py:48
  50.0 21.5 %all_gather.6 = s32[16384]{0:T(1024)S(1)} all-gather(s32[1024]{0:T(1024)S(1)} %reshape.75), channel_id=1, replica_groups=mesh['shard'=8,'split'=16] {'split'}, dimensions={0}, use_global_device_ids=true | all-gather | bytes 69632 | tf_op jit(solution)/shard_map/all_gather | solution.py:63
  71.6 77.9 %all-gather.2.cloned.1.call-done = bf16[16384,512]{1,0:T(8,128)(2,1)} async-done(((bf16[1024,512]{1,0:T(8,128)(2,1)}), bf16[16384,512]{1,0:T(8,128)(2,1)}) %all-gather.2.cloned.1.call-update) | async-done | bytes 16777232 | tf_op jit(solution)/shard_map/all_gather | solution.py:62
  149.4 48.1 %while.12 = (s32[]{:T(128)}, f32[1024]{0:T(1024)S(1)}, s32[16,1024]{1,0:T(8,128)S(1)}, s32[4,8,32]{2,1,0:T(8,128)}, bf16[16,1024,512]{2,1,0:T(8,128)(2,1)}, /*in...) while((s32[]{:T(128)}, f32[1024]{0:T(1024)S(1)}, ...), condition=%wide.wide.region_8.9_spmd.clone, body=%wide.wide.region_6.8_spmd.clone.sunk | while | flops 1078985728 | bytes 2138739 | solution.py:71
  149.5 2.9 %fusion.36 = f32[1024]{0:T(1024)S(1)} fusion(bf16[1024,512]{1,0:T(8,128)(2,1)} %get-tuple-element.200, s32[1024]{0:T(1024)S(1)} %get-tuple-element.201, s32[1024]{0:T(1024)S(1)} %get-tuple-element.202, s32[1024]{0:T(1024)S(1)} %bitcast.55, bf16[16,1024,512]{2,1,0:T(8,128)(2,1)} %get-tuple-element.199, s32[]{:T(128)} %get-tuple-element.185), kind=kOutput, calls=%fused_computation.5.clone.clone.1 | convolution fusion | flops 1078983680 | bytes 2118144 | tf_op jit(solution)/shard_map/while/body/eval_jaxpr/dot_general | solution.py:13
  152.5 2.9 %fusion.36 = f32[1024]{0:T(1024)S(1)} fusion(bf16[1024,512]{1,0:T(8,128)(2,1)} %get-tuple-element.200, s32[1024]{0:T(1024)S(1)} %get-tuple-element.201, s32[1024]{0:T(1024)S(1)} %get-tuple-element.202, s32[1024]{0:T(1024)S(1)} %bitcast.55, bf16[16,1024,512]{2,1,0:T(8,128)(2,1)} %get-tuple-element.199, s32[]{:T(128)} %get-tuple-element.185), kind=kOutput, calls=%fused_computation.5.clone.clone.1 | convolution fusion | flops 1078983680 | bytes 2118144 | tf_op jit(solution)/shard_map/while/body/eval_jaxpr/dot_general | solution.py:13
  155.5 3.0 %fusion.36 = f32[1024]{0:T(1024)S(1)} fusion(bf16[1024,512]{1,0:T(8,128)(2,1)} %get-tuple-element.200, s32[1024]{0:T(1024)S(1)} %get-tuple-element.201, s32[1024]{0:T(1024)S(1)} %get-tuple-element.202, s32[1024]{0:T(1024)S(1)} %bitcast.55, bf16[16,1024,512]{2,1,0:T(8,128)(2,1)} %get-tuple-element.199, s32[]{:T(128)} %get-tuple-element.185), kind=kOutput, calls=%fused_computation.5.clone.clone.1 | convolution fusion | flops 1078983680 | bytes 2118144 | tf_op jit(solution)/shard_map/while/body/eval_jaxpr/dot_general | solution.py:13
  158.5 2.9 %fusion.36 = f32[1024]{0:T(1024)S(1)} fusion(bf16[1024,512]{1,0:T(8,128)(2,1)} %get-tuple-element.200, s32[1024]{0:T(1024)S(1)} %get-tuple-element.201, s32[1024]{0:T(1024)S(1)} %get-tuple-element.202, s32[1024]{0:T(1024)S(1)} %bitcast.55, bf16[16,1024,512]{2,1,0:T(8,128)(2,1)} %get-tuple-element.199, s32[]{:T(128)} %get-tuple-element.185), kind=kOutput, calls=%fused_computation.5.clone.clone.1 | convolution fusion | flops 1078983680 | bytes 2118144 | tf_op jit(solution)/shard_map/while/body/eval_jaxpr/dot_general | solution.py:13
  161.5 3.0 %fusion.36 = f32[1024]{0:T(1024)S(1)} fusion(bf16[1024,512]{1,0:T(8,128)(2,1)} %get-tuple-element.200, s32[1024]{0:T(1024)S(1)} %get-tuple-element.201, s32[1024]{0:T(1024)S(1)} %get-tuple-element.202, s32[1024]{0:T(1024)S(1)} %bitcast.55, bf16[16,1024,512]{2,1,0:T(8,128)(2,1)} %get-tuple-element.199, s32[]{:T(128)} %get-tuple-element.185), kind=kOutput, calls=%fused_computation.5.clone.clone.1 | convolution fusion | flops 1078983680 | bytes 2118144 | tf_op jit(solution)/shard_map/while/body/eval_jaxpr/dot_general | solution.py:13
  164.5 2.9 %fusion.36 = f32[1024]{0:T(1024)S(1)} fusion(bf16[1024,512]{1,0:T(8,128)(2,1)} %get-tuple-element.200, s32[1024]{0:T(1024)S(1)} %get-tuple-element.201, s32[1024]{0:T(1024)S(1)} %get-tuple-element.202, s32[1024]{0:T(1024)S(1)} %bitcast.55, bf16[16,1024,512]{2,1,0:T(8,128)(2,1)} %get-tuple-element.199, s32[]{:T(128)} %get-tuple-element.185), kind=kOutput, calls=%fused_computation.5.clone.clone.1 | convolution fusion | flops 1078983680 | bytes 2118144 | tf_op jit(solution)/shard_map/while/body/eval_jaxpr/dot_general | solution.py:13
  167.5 3.0 %fusion.36 = f32[1024]{0:T(1024)S(1)} fusion(bf16[1024,512]{1,0:T(8,128)(2,1)} %get-tuple-element.200, s32[1024]{0:T(1024)S(1)} %get-tuple-element.201, s32[1024]{0:T(1024)S(1)} %get-tuple-element.202, s32[1024]{0:T(1024)S(1)} %bitcast.55, bf16[16,1024,512]{2,1,0:T(8,128)(2,1)} %get-tuple-element.199, s32[]{:T(128)} %get-tuple-element.185), kind=kOutput, calls=%fused_computation.5.clone.clone.1 | convolution fusion | flops 1078983680 | bytes 2118144 | tf_op jit(solution)/shard_map/while/body/eval_jaxpr/dot_general | solution.py:13
  170.5 2.9 %fusion.36 = f32[1024]{0:T(1024)S(1)} fusion(bf16[1024,512]{1,0:T(8,128)(2,1)} %get-tuple-element.200, s32[1024]{0:T(1024)S(1)} %get-tuple-element.201, s32[1024]{0:T(1024)S(1)} %get-tuple-element.202, s32[1024]{0:T(1024)S(1)} %bitcast.55, bf16[16,1024,512]{2,1,0:T(8,128)(2,1)} %get-tuple-element.199, s32[]{:T(128)} %get-tuple-element.185), kind=kOutput, calls=%fused_computation.5.clone.clone.1 | convolution fusion | flops 1078983680 | bytes 2118144 | tf_op jit(solution)/shard_map/while/body/eval_jaxpr/dot_general | solution.py:13
  173.5 3.0 %fusion.36 = f32[1024]{0:T(1024)S(1)} fusion(bf16[1024,512]{1,0:T(8,128)(2,1)} %get-tuple-element.200, s32[1024]{0:T(1024)S(1)} %get-tuple-element.201, s32[1024]{0:T(1024)S(1)} %get-tuple-element.202, s32[1024]{0:T(1024)S(1)} %bitcast.55, bf16[16,1024,512]{2,1,0:T(8,128)(2,1)} %get-tuple-element.199, s32[]{:T(128)} %get-tuple-element.185), kind=kOutput, calls=%fused_computation.5.clone.clone.1 | convolution fusion | flops 1078983680 | bytes 2118144 | tf_op jit(solution)/shard_map/while/body/eval_jaxpr/dot_general | solution.py:13
  176.5 2.9 %fusion.36 = f32[1024]{0:T(1024)S(1)} fusion(bf16[1024,512]{1,0:T(8,128)(2,1)} %get-tuple-element.200, s32[1024]{0:T(1024)S(1)} %get-tuple-element.201, s32[1024]{0:T(1024)S(1)} %get-tuple-element.202, s32[1024]{0:T(1024)S(1)} %bitcast.55, bf16[16,1024,512]{2,1,0:T(8,128)(2,1)} %get-tuple-element.199, s32[]{:T(128)} %get-tuple-element.185), kind=kOutput, calls=%fused_computation.5.clone.clone.1 | convolution fusion | flops 1078983680 | bytes 2118144 | tf_op jit(solution)/shard_map/while/body/eval_jaxpr/dot_general | solution.py:13
  179.6 3.0 %fusion.36 = f32[1024]{0:T(1024)S(1)} fusion(bf16[1024,512]{1,0:T(8,128)(2,1)} %get-tuple-element.200, s32[1024]{0:T(1024)S(1)} %get-tuple-element.201, s32[1024]{0:T(1024)S(1)} %get-tuple-element.202, s32[1024]{0:T(1024)S(1)} %bitcast.55, bf16[16,1024,512]{2,1,0:T(8,128)(2,1)} %get-tuple-element.199, s32[]{:T(128)} %get-tuple-element.185), kind=kOutput, calls=%fused_computation.5.clone.clone.1 | convolution fusion | flops 1078983680 | bytes 2118144 | tf_op jit(solution)/shard_map/while/body/eval_jaxpr/dot_general | solution.py:13
  185.6 3.0 %fusion.36 = f32[1024]{0:T(1024)S(1)} fusion(bf16[1024,512]{1,0:T(8,128)(2,1)} %get-tuple-element.200, s32[1024]{0:T(1024)S(1)} %get-tuple-element.201, s32[1024]{0:T(1024)S(1)} %get-tuple-element.202, s32[1024]{0:T(1024)S(1)} %bitcast.55, bf16[16,1024,512]{2,1,0:T(8,128)(2,1)} %get-tuple-element.199, s32[]{:T(128)} %get-tuple-element.185), kind=kOutput, calls=%fused_computation.5.clone.clone.1 | convolution fusion | flops 1078983680 | bytes 2118144 | tf_op jit(solution)/shard_map/while/body/eval_jaxpr/dot_general | solution.py:13
  188.6 2.9 %fusion.36 = f32[1024]{0:T(1024)S(1)} fusion(bf16[1024,512]{1,0:T(8,128)(2,1)} %get-tuple-element.200, s32[1024]{0:T(1024)S(1)} %get-tuple-element.201, s32[1024]{0:T(1024)S(1)} %get-tuple-element.202, s32[1024]{0:T(1024)S(1)} %bitcast.55, bf16[16,1024,512]{2,1,0:T(8,128)(2,1)} %get-tuple-element.199, s32[]{:T(128)} %get-tuple-element.185), kind=kOutput, calls=%fused_computation.5.clone.clone.1 | convolution fusion | flops 1078983680 | bytes 2118144 | tf_op jit(solution)/shard_map/while/body/eval_jaxpr/dot_general | solution.py:13
  191.6 3.0 %fusion.36 = f32[1024]{0:T(1024)S(1)} fusion(bf16[1024,512]{1,0:T(8,128)(2,1)} %get-tuple-element.200, s32[1024]{0:T(1024)S(1)} %get-tuple-element.201, s32[1024]{0:T(1024)S(1)} %get-tuple-element.202, s32[1024]{0:T(1024)S(1)} %bitcast.55, bf16[16,1024,512]{2,1,0:T(8,128)(2,1)} %get-tuple-element.199, s32[]{:T(128)} %get-tuple-element.185), kind=kOutput, calls=%fused_computation.5.clone.clone.1 | convolution fusion | flops 1078983680 | bytes 2118144 | tf_op jit(solution)/shard_map/while/body/eval_jaxpr/dot_general | solution.py:13
  198.4 5.0 %all-to-all-start.2 = ((f32[8,1,128]{2,1,0:T(1,128)}), f32[8,1,128]{2,1,0:T(1,128)S(1)}, u32[]{:S(2)}, u32[]{:S(2)}) async-start(f32[8,1,128]{2,1,0:T(1,128)} %reshape.116), calls=%async_computation.2 | async-start | bytes 8192 | tf_op jit(solution)/shard_map/all_to_all | solution.py:76
  203.3 4.6 %all-to-all-done.2 = f32[8,1,128]{2,1,0:T(1,128)S(1)} async-done(((f32[8,1,128]{2,1,0:T(1,128)}), f32[8,1,128]{2,1,0:T(1,128)S(1)}, u32[]{:S(2)}, u32[]{:S(2)}) %all-to-all-start.2) | async-done | bytes 4128 | tf_op jit(solution)/shard_map/all_to_all | solution.py:76
  209.2 3.4 %gather_fusion = f32[512]{0:T(512)} fusion(f32[1024]{0:T(1024)S(1)} %reshape.81, s32[1024]{0:T(1024)S(1)} %pad_clamp_fusion), kind=kCustom, calls=%fused_computation | custom fusion | bytes 6144 | tf_op jit(solution)/shard_map/gather | solution.py:83
  (71 shorter events, 19.0 us)
Async XLA Ops:
  6.5 142.9 %all-gather.2.cloned.1.call-start = ((), (), s32[]{:S(2)}) async-start(), calls=%async_computation.3 | async-start | bytes 17825792 | tf_op jit(solution)/shard_map/all_gather | solution.py:62
  39.9 8.8 %all-to-all-start = ((s32[8,1,128]{2,1,0:T(1,128)}), s32[8,1,128]{2,1,0:T(1,128)S(1)}, u32[]{:S(2)}, u32[]{:S(2)}) async-start(s32[8,1,128]{2,1,0:T(1,128)} %reshape.114), calls=%async_computation | async-start | bytes 8192 | tf_op jit(solution)/shard_map/all_to_all | solution.py:48
  49.9 99.6 %copy-start = (s32[4,8,32]{2,1,0:T(8,128)}, s32[4,8,32]{2,1,0:T(8,128)S(1)}, u32[]{:S(2)}) copy-start(s32[4,8,32]{2,1,0:T(8,128)S(1)} %copy.10) | copy-start | bytes 12292
  198.4 9.5 %all-to-all-start.2 = ((f32[8,1,128]{2,1,0:T(1,128)}), f32[8,1,128]{2,1,0:T(1,128)S(1)}, u32[]{:S(2)}, u32[]{:S(2)}) async-start(f32[8,1,128]{2,1,0:T(1,128)} %reshape.116), calls=%async_computation.2 | async-start | bytes 8192 | tf_op jit(solution)/shard_map/all_to_all | solution.py:76
Sparse Core Ops, SparseCore 0:
  36.6 112.7 all-gather.1
where the time goes:
time: 220 us; the launch traced here: 219 us
  waiting for transfers between devices  87 us (40%)
  matrix products  47.2 us (21%)
  blocking collectives  42.2 us (19%)
  between operations  13.5 us (6%)
  local copies, waits for them, and re-layouts  10.5 us (5%)
  other arithmetic  9.22 us (4%)
  starting transfers between devices  9.17 us (4%)
    all_gather x1, waiting for transfers between devices, body(): piece_rows = lax.all_gather(row_block, 'split', axis=0, tiled=True)  77.9 us
    dot_general x16, matrix products, masked_best(): lax.dot_general(row_block, col_block, (((1,), (1,)), ((), ())), preferred...  47.2 us
    all_gather x1, blocking collectives, body(): piece_rank = lax.all_gather(row_rank, 'split', axis=0, tiled=True)  21.5 us
    all_to_all x1, blocking collectives, body(): lax.all_to_all(outgoing.reshape(CL_PER, shard_count, per_cluster, width),...  20.7 us
    all_to_all x1, starting transfers between devices, body(): lax.all_to_all(carry.reshape(CL_PER, shard_count, per_cluster), 'shard',...  4.96 us
    all_to_all x1, waiting for transfers between devices, body(): lax.all_to_all(out_rank.reshape(CL_PER, shard_count, per_cluster), 'shard...  4.58 us
    all_to_all x1, waiting for transfers between devices, body(): lax.all_to_all(carry.reshape(CL_PER, shard_count, per_cluster), 'shard',...  4.57 us
  transfers between devices with their start and end apart: 3, of which 3 were waited for; matrix products, arithmetic and copies ran while one was open for 2% of the time, Pallas kernels for 0%

commit v1 on v0

v1 whole, which is shorter than its diff:
```python
import jax
import jax.numpy as jnp
from jax import lax
from jax.experimental import pallas as pl
from jax.experimental.pallas import tpu as pltpu
from jax.sharding import PartitionSpec as P

MESH = pl.DeviceIdType.MESH
CLUSTERS = 32
SLOTS = 32
CHIPS = 64
BLOCK = 256
BLOCKS = 8
NO_RANK = float(1 << 30)


def place(x, y, z, core):
    return (2 * x + core, 4 * z + y)


def kernel(
    embedding_ref, cluster_ref, rank_ref, out_ref,
    outgoing, out_rank, members, member_rank, rank_column, rank_row, best, back,
    send_sem, rank_send_sem, member_sem, rank_sem, pair_send_sem, pair_rank_send_sem, pair_sem, pair_rank_sem,
    back_send_sem, back_sem,
):
    shard, split = lax.axis_index("shard"), lax.axis_index("split")
    x, core, z, y = shard // 2, shard % 2, split // 4, split % 4
    chip = x + 4 * y + 16 * z
    group = chip // 4
    holds = (x + y + z) % 2 == 0
    own = x + 4 * y + 16 * (z // 2)
    rows = embedding_ref.shape[0]

    barrier = pltpu.get_barrier_semaphore()

    @pl.when(holds)
    def _():
        def greet(s, carry):
            pl.semaphore_signal(
                barrier, inc=1, device_id=place(s % 4, (s // 4) % 4, s // 16, core), device_id_type=MESH
            )
            return carry

        lax.fori_loop(0, CHIPS, greet, 0)
        pl.semaphore_signal(barrier, inc=1, device_id=place(x, y, z, 1 - core), device_id_type=MESH)

    values = embedding_ref[...].astype(jnp.float32)
    unit = (
        values * lax.rsqrt(jnp.sum(values * values, axis=1, keepdims=True) + 1e-06)
    ).astype(jnp.bfloat16)
    cluster = cluster_ref[...]
    rank = rank_ref[...]
    cluster_hit = lax.broadcasted_iota(jnp.int32, (CLUSTERS, rows), 0) == cluster
    onehot = cluster_hit.astype(jnp.float32)
    earlier = (
        lax.broadcasted_iota(jnp.int32, (rows, rows), 0) < lax.broadcasted_iota(jnp.int32, (rows, rows), 1)
    ).astype(jnp.float32).astype(jnp.bfloat16)
    before = jnp.dot(onehot.astype(jnp.bfloat16), earlier, preferred_element_type=jnp.float32)
    position = jnp.sum(before * onehot, axis=0, keepdims=True).astype(jnp.int32)
    slot = cluster * SLOTS + position

    def fill(part, carry):
        base = part * 256
        pick = (lax.broadcasted_iota(jnp.int32, (256, rows), 0) + base == slot).astype(jnp.float32).astype(jnp.bfloat16)
        packed = jnp.dot(pick, unit, preferred_element_type=jnp.float32).astype(jnp.bfloat16)
        outgoing[pl.ds(part * 8, 8)] = packed.reshape(8, SLOTS, packed.shape[1])
        return carry

    lax.fori_loop(0, CLUSTERS * SLOTS // 256, fill, 0)

    lane = lax.broadcasted_iota(jnp.int32, (128, rows), 0)
    lane_hit = (lane == position + SLOTS * x).astype(jnp.float32).astype(jnp.bfloat16)
    contract_last = (((1,), (1,)), ((), ()))

    def spread(part):
        return lax.dot_general(
            (onehot * part.astype(jnp.float32)).astype(jnp.bfloat16), lane_hit, contract_last,
            preferred_element_type=jnp.float32,
        )

    taken = spread(jnp.ones_like(rank))
    slot_rank = (
        spread(rank % 128) + 128.0 * spread(rank // 128 % 128) + 16384.0 * spread(rank // 16384)
    )
    mine = lax.broadcasted_iota(jnp.int32, (CLUSTERS, 128), 1) // SLOTS == x
    out_rank[...] = jnp.where(mine, jnp.where(taken > 0.5, slot_rank, NO_RANK), 0.0).reshape(CLUSTERS, 1, 128)

    pl.semaphore_wait(barrier, CLUSTERS + jnp.where(holds, 1, 0))

    block = chip // 8
    slot_in_block = chip % 8

    def send(t, carry):
        c = (t + chip // 2) % CLUSTERS
        cx, cy = c % 4, (c // 4) % 4
        cz = 2 * (c // 16) + (cx + cy) % 2
        here = (cx == x) & (cy == y) & (cz == z)

        @pl.when(jnp.logical_not(here))
        def _():
            pltpu.make_async_remote_copy(
                out_rank.at[c], member_rank.at[0, block, slot_in_block], rank_send_sem, rank_sem.at[block],
                device_id=place(cx, cy, cz, core), device_id_type=MESH,
            ).start()
            pltpu.make_async_remote_copy(
                outgoing.at[c], members.at[0, block, pl.ds(pl.multiple_of(slot_in_block * SLOTS, SLOTS), SLOTS)],
                send_sem, member_sem.at[block], device_id=place(cx, cy, cz, core), device_id_type=MESH,
            ).start()

        @pl.when(here)
        def _():
            pltpu.make_async_copy(
                out_rank.at[c], member_rank.at[0, block, slot_in_block], rank_sem.at[block]
            ).start()
            pltpu.make_async_copy(
                outgoing.at[c], members.at[0, block, pl.ds(pl.multiple_of(slot_in_block * SLOTS, SLOTS), SLOTS)],
                member_sem.at[block],
            ).start()

        return carry

    lax.fori_loop(0, CLUSTERS, send, 0)

    def arrived(ref, sem):
        pltpu.make_async_copy(ref, ref, sem).wait()

    @pl.when(holds)
    def _():
        best[...] = jnp.full(best.shape, -1.0, jnp.float32)

        def tile(side, j, i):
            scores = lax.dot_general(
                members[side, j], members[0, i], contract_last, preferred_element_type=jnp.float32
            )
            lower = jnp.concatenate([rank_column[side, j], rank_column[side, j]], axis=1) < rank_row[i]
            found = jnp.where(lower, scores, -1.0).reshape(BLOCK // 8, 8, BLOCK)
            best[i] = jnp.maximum(best[i], jnp.max(found, axis=0))

        def ranks(side, b):
            eight = member_rank[side, b].reshape(8, 128)
            halves = [jnp.sum(eight[4 * h : 4 * h + 4], axis=0, keepdims=True) for h in range(2)]
            if side == 0:
                rank_row[b] = jnp.concatenate(halves, axis=1)
            for h in range(2):
                rank_column[side, b, pl.ds(128 * h, 128)] = jnp.broadcast_to(halves[h], (128, 128)).T

        def step(b, carry):
            arrived(member_rank.at[0, b], rank_sem.at[b])
            arrived(members.at[0, b], member_sem.at[b])
            sibling = place(x, y, z, 1 - core)
            pltpu.make_async_remote_copy(
                member_rank.at[0, b], member_rank.at[1, b], pair_rank_send_sem, pair_rank_sem.at[b],
                device_id=sibling, device_id_type=MESH,
            ).start()
            pltpu.make_async_remote_copy(
                members.at[0, b], members.at[1, b], pair_send_sem, pair_sem.at[b],
                device_id=sibling, device_id_type=MESH,
            ).start()
            ranks(0, b)
            lax.fori_loop(0, b + 1, lambda j, c: (tile(0, j, b), c)[1], 0)
            lax.fori_loop(0, b, lambda i, c: (tile(0, b, i), c)[1], 0)
            arrived(member_rank.at[1, b], pair_rank_sem.at[b])
            arrived(members.at[1, b], pair_sem.at[b])
            ranks(1, b)
            lax.fori_loop(0, b + 1, lambda j, c: (tile(1, j, b), c)[1], 0)
            lax.fori_loop(0, b, lambda i, c: (tile(1, b, i), c)[1], 0)
            return carry

        lax.fori_loop(0, BLOCKS, step, 0)

        def reply(s, carry):
            sx, sy, sz = s % 4, (s // 4) % 4, s // 16
            here = s == chip
            lanes = pl.ds(pl.multiple_of(sy % 2 * 128, 128), 128)

            @pl.when(jnp.logical_not(here))
            def _():
                pltpu.make_async_remote_copy(
                    best.at[s // 8, :, lanes], back.at[own], back_send_sem, back_sem,
                    device_id=place(sx, sy, sz, core), device_id_type=MESH,
                ).start()

            @pl.when(here)
            def _():
                pltpu.make_async_copy(best.at[s // 8, :, lanes], back.at[own], back_sem).start()

            return carry

        lax.fori_loop(0, CHIPS, reply, 0)

    arrived(back, back_sem)
    table = jnp.max(back[...], axis=1)
    column = lax.broadcasted_iota(jnp.int32, (128, rows), 0) == position + SLOTS * x
    found = lax.dot_general(
        table, onehot, (((0,), (0,)), ((), ())),
        precision=lax.Precision.HIGHEST, preferred_element_type=jnp.float32,
    )
    out_ref[...] = jnp.sum(jnp.where(column, found, 0.0), axis=0, keepdims=True)

    @pl.when(holds)
    def _():
        arrived(outgoing.at[pl.ds(0, CLUSTERS - 1)], send_sem)
        arrived(out_rank.at[pl.ds(0, CLUSTERS - 1)], rank_send_sem)
        arrived(members.at[0], pair_send_sem)
        arrived(member_rank.at[0], pair_rank_send_sem)
        arrived(back, back_send_sem)
        arrived(back.at[pl.ds(0, CLUSTERS - 1)], back_send_sem)

    @pl.when(jnp.logical_not(holds))
    def _():
        arrived(outgoing, send_sem)
        arrived(out_rank, rank_send_sem)


def body(embedding, cluster, rank):
    rows, width = embedding.shape
    vmem = pl.BlockSpec(memory_space=pltpu.VMEM)
    dma = pltpu.SemaphoreType.DMA
    found = pl.pallas_call(
        kernel,
        out_shape=jax.ShapeDtypeStruct((1, rows), jnp.float32),
        in_specs=[vmem] * 3,
        out_specs=vmem,
        scratch_shapes=[
            pltpu.VMEM((CLUSTERS, SLOTS, width), jnp.bfloat16),
            pltpu.VMEM((CLUSTERS, 1, 128), jnp.float32),
            pltpu.VMEM((2, BLOCKS, BLOCK, width), jnp.bfloat16),
            pltpu.VMEM((2, BLOCKS, 8, 1, 128), jnp.float32),
            pltpu.VMEM((2, BLOCKS, BLOCK, 128), jnp.float32),
            pltpu.VMEM((BLOCKS, 1, BLOCK), jnp.float32),
            pltpu.VMEM((BLOCKS, 8, BLOCK), jnp.float32),
            pltpu.VMEM((CLUSTERS, 8, 128), jnp.float32),
            dma, dma, dma((BLOCKS,)), dma((BLOCKS,)), dma, dma, dma((BLOCKS,)), dma((BLOCKS,)), dma, dma,
        ],
        compiler_params=pltpu.CompilerParams(
            collective_id=0, has_side_effects=True, vmem_limit_bytes=48 << 20
        ),
    )(embedding, cluster.reshape(1, rows), rank.reshape(1, rows))
    return found.reshape(rows)


def solution(mesh):
    return jax.shard_map(
        body,
        mesh=mesh,
        in_specs=(P(("shard", "split"), None), P(("shard", "split")), P(("shard", "split"))),
        out_specs=P(("shard", "split")),
        check_vma=False,
    )
```

time: 220 us -> 81.8 us (0.37)
  waiting for transfers between devices: 87 us -> 0 us
  Pallas kernels: 0 us -> 78.6 us
  matrix products: 47.2 us -> 0 us
  blocking collectives: 42.2 us -> 0 us
  between operations: 13.5 us -> 0.01 us
  other arithmetic: 9.22 us -> 0 us
  starting transfers between devices: 9.17 us -> 0 us
  local copies, waits for them, and re-layouts: 10.5 us -> 2.98 us
    pallas_call x0 -> x1, Pallas kernels: none -> 78.6 us  [body(): pl.pallas_call(kernel, out_shape=jax.ShapeDtypeStruct((1, rows), jnp.floa...]
    all_gather x1 -> x0, waiting for transfers between devices: 77.9 us -> none  [body(): piece_rows = lax.all_gather(row_block, 'split', axis=0, tiled=True)]
    dot_general x16 -> x0, matrix products: 47.2 us -> none  [masked_best(): lax.dot_general(row_block, col_block, (((1,), (1,)), ((), ())), preferred...]
    all_gather x1 -> x0, blocking collectives: 21.5 us -> none  [body(): piece_rank = lax.all_gather(row_rank, 'split', axis=0, tiled=True)]
    all_to_all x1 -> x0, blocking collectives: 20.7 us -> none  [body(): lax.all_to_all(outgoing.reshape(CL_PER, shard_count, per_cluster, width),...]
    all_to_all x2 -> x0, starting transfers between devices: 9.16 us -> none  [the longest x1 4.96 us: body(): lax.all_to_all(carry.reshape(CL_PER, shard_count, per_cluster), 'shard',...]
    all_to_all x2 -> x0, waiting for transfers between devices: 9.15 us -> none  [the longest x1 4.58 us: body(): lax.all_to_all(out_rank.reshape(CL_PER, shard_count, per_cluster), 'shard...]
    gather x1 -> x0, local copies, waits for them, and re-layouts: 3.41 us -> none  [body(): return returned.reshape(slot_count)[slot]]
  transfers between devices with their start and end apart: 3 -> 0, of which waited for: 3 -> 0; matrix products, arithmetic and copies ran while one was open for 2% -> 0% of each run, Pallas kernels for 0% -> 0%
where the time goes in v1:
time: 81.8 us; the launch traced here: 81.6 us
  Pallas kernels  78.6 us (96%)
  local copies, waits for them, and re-layouts  2.98 us (4%)
    pallas_call x1, Pallas kernels, body(): pl.pallas_call(kernel, out_shape=jax.ShapeDtypeStruct((1, rows), jnp.floa...  78.6 us
    unnamed x7, local copies, waits for them, and re-layouts  2.98 us

profile of v1, /device:TPU:1, one launch (start us, length us, event | category | flops | bytes accessed | tf_op | source)
XLA Modules:
  0.0 81.6 jit_solution(9609795397882988798)
XLA Ops:
  0.0 0.0 copy-start.1
  0.0 0.7 copy-done.1
  0.7 0.0 copy-start
  0.7 1.0 %copy-done = bf16[512,512]{1,0:T(8,128)(2,1)S(1)} copy-done((bf16[512,512]{1,0:T(8,128)(2,1)S(1)}, bf16[512,512]{1,0:T(8,128)(2,1)}, u32[]{:S(2)}) %copy-start) | copy-done | bytes 524312
  1.7 0.0 copy-start.2
  1.7 0.7 copy-done.2
  2.4 78.6 %shard_map.37 = f32[1,512]{1,0:T(1,128)S(1)} custom-call(bf16[512,512]{1,0:T(8,128)(2,1)S(1)} %copy-done, s32[1,512]{1,0:T(1,128)S(1)} %bitcast.4, s32[1,512]{1,0:T(1,128)S(1)} %bitcast.5), custom_call_target="tpu_custom_call" | custom-call | tf_op jit(solution)/shard_map/pallas_call | solution.py:220
  81.0 0.6 copy.5
Async XLA Ops:
  0.0 0.7 copy-start.1
  0.7 1.0 %copy-start = (bf16[512,512]{1,0:T(8,128)(2,1)S(1)}, bf16[512,512]{1,0:T(8,128)(2,1)}, u32[]{:S(2)}) copy-start(bf16[512,512]{1,0:T(8,128)(2,1)} %embedding_ref.1) | copy-start | bytes 1572868
  1.7 0.7 copy-start.2

commit v2 on v1

v2 whole, which is shorter than its diff:
```python
import jax
import jax.numpy as jnp
from jax import lax
from jax.experimental import pallas as pl
from jax.experimental.pallas import tpu as pltpu
from jax.sharding import PartitionSpec as P

MESH = pl.DeviceIdType.MESH
CLUSTERS = 32
SLOTS = 32
GROUP = 4 * SLOTS
GROUPS = 16
PARITY = 1
NO_RANK = float(1 << 30)
ORDER = [
    (1, 2), (3, 2), (2, 2), (0, 2), (2, 1), (2, 3), (1, 1), (3, 3),
    (3, 1), (1, 3), (0, 1), (0, 3), (2, 0), (1, 0), (3, 0), (0, 0),
]
RELAYED = [(1, 2), (3, 2)]
STEPS = [4, 4, 4, 2, 1, 1]
STARTS = [sum(STEPS[:k]) for k in range(len(STEPS) + 1)]


def place(x, y, z, core):
    return (2 * x + core, 4 * z + y)


def step_of(t):
    return max(k for k in range(len(STEPS)) if STARTS[k] <= t)


def arrived(ref, sem):
    pltpu.make_async_copy(ref, ref, sem).wait()


def remote(src, dst, send_sem, recv_sem, target):
    return pltpu.make_async_remote_copy(
        src, dst, send_sem, recv_sem, device_id=target, device_id_type=MESH
    )


def kernel(
    embedding_ref, cluster_ref, rank_ref, out_ref,
    outgoing, out_rank, passing, passing_rank, members, member_rank, rank_column, rank_row, best, back,
    send_sem, rank_send_sem, pass_sem, pass_rank_sem, pass_send_sem, pass_rank_send_sem, member_sem, rank_sem,
    pair_send_sem, pair_rank_send_sem, pair_sem, pair_rank_sem, back_send_sem, back_sem,
):
    shard, split = lax.axis_index("shard"), lax.axis_index("split")
    x, core, z, y = shard // 2, shard % 2, split // 4, split % 4
    holds = (x + y + z) % 2 == PARITY
    own = x + 4 * y + 16 * (z // 2)
    rows = embedding_ref.shape[0]

    barrier = pltpu.get_barrier_semaphore()

    def greet(gx, gy, gz, gcore):
        pl.semaphore_signal(barrier, inc=1, device_id=place(gx, gy, gz, gcore), device_id_type=MESH)

    @pl.when(holds)
    def _():
        def each(s, carry):
            greet(s % 4, (s // 4) % 4, s // 16, core)
            return carry

        lax.fori_loop(0, 64, each, 0)
        greet(x, y, z, 1 - core)

    @pl.when(jnp.logical_not(holds))
    def _():
        for sy in range(4):
            greet(x, sy, (z + 2) % 4, core)

    values = embedding_ref[...].astype(jnp.float32)
    unit = (
        values * lax.rsqrt(jnp.sum(values * values, axis=1, keepdims=True) + 1e-06)
    ).astype(jnp.bfloat16)
    cluster = cluster_ref[...]
    rank = rank_ref[...]
    cluster_hit = lax.broadcasted_iota(jnp.int32, (CLUSTERS, rows), 0) == cluster
    onehot = cluster_hit.astype(jnp.float32)
    earlier = (
        lax.broadcasted_iota(jnp.int32, (rows, rows), 0) < lax.broadcasted_iota(jnp.int32, (rows, rows), 1)
    ).astype(jnp.float32).astype(jnp.bfloat16)
    before = jnp.dot(onehot.astype(jnp.bfloat16), earlier, preferred_element_type=jnp.float32)
    position = jnp.sum(before * onehot, axis=0, keepdims=True).astype(jnp.int32)
    slot = cluster * SLOTS + position

    def fill(part, carry):
        pick = (
            lax.broadcasted_iota(jnp.int32, (256, rows), 0) + part * 256 == slot
        ).astype(jnp.float32).astype(jnp.bfloat16)
        packed = jnp.dot(pick, unit, preferred_element_type=jnp.float32).astype(jnp.bfloat16)
        outgoing[pl.ds(part * 8, 8)] = packed.reshape(8, SLOTS, packed.shape[1])
        return carry

    lax.fori_loop(0, CLUSTERS * SLOTS // 256, fill, 0)

    lane_hit = lax.broadcasted_iota(jnp.int32, (GROUP, rows), 0) == position + SLOTS * y
    lane_onehot = lane_hit.astype(jnp.float32).astype(jnp.bfloat16)
    contract_last = (((1,), (1,)), ((), ()))

    def spread(part):
        return lax.dot_general(
            (onehot * part.astype(jnp.float32)).astype(jnp.bfloat16), lane_onehot, contract_last,
            preferred_element_type=jnp.float32,
        )

    taken = spread(jnp.ones_like(rank))
    slot_rank = (
        spread(rank % 128) + 128.0 * spread(rank // 128 % 128) + 16384.0 * spread(rank // 16384)
    )
    mine = lax.broadcasted_iota(jnp.int32, (CLUSTERS, GROUP), 1) // SLOTS == y
    out_rank[...] = jnp.where(mine, jnp.where(taken > 0.5, slot_rank, NO_RANK), 0.0).reshape(CLUSTERS, 1, GROUP)

    pl.semaphore_wait(barrier, CLUSTERS + 2 + jnp.where(holds, 1, 0))

    for t, (dx, dz) in enumerate(ORDER):
        ax, az = (x + 4 - dx) % 4, (z + 4 - dz) % 4
        for half in range(2):
            ay = (y + (ax + y + az + PARITY) % 2 + 2 * half) % 4
            c = ax + 4 * ay + 16 * (az // 2)
            if (dx, dz) in RELAYED:
                side = RELAYED.index((dx, dz))
                target = place(x, ay, az, core)
                remote(
                    out_rank.at[c], passing_rank.at[side, y], rank_send_sem, pass_rank_sem.at[side], target
                ).start()
                remote(outgoing.at[c], passing.at[side, y], send_sem, pass_sem.at[side], target).start()
                continue
            k = step_of(t)
            rank_there, rank_there_sem = member_rank.at[0, t, y], rank_sem.at[k]
            there = members.at[0, pl.ds(pl.multiple_of(t * GROUP + y * SLOTS, SLOTS), SLOTS)]
            there_sem = member_sem.at[k]
            target = place(ax, ay, az, core)

            def away():
                remote(out_rank.at[c], rank_there, rank_send_sem, rank_there_sem, target).start()
                remote(outgoing.at[c], there, send_sem, there_sem, target).start()

            if (dx, dz) == (0, 0):
                pl.when(ay != y)(away)

                @pl.when(ay == y)
                def _():
                    pltpu.make_async_copy(out_rank.at[c], rank_there, rank_there_sem).start()
                    pltpu.make_async_copy(outgoing.at[c], there, there_sem).start()
            else:
                away()

    @pl.when(jnp.logical_not(holds))
    def _():
        for side, (dx, dz) in enumerate(RELAYED):
            t = ORDER.index((dx, dz))
            k = step_of(t)
            target = place((x + 4 - dx) % 4, y, z, core)
            arrived(passing_rank.at[side], pass_rank_sem.at[side])
            remote(
                passing_rank.at[side], member_rank.at[0, t], pass_rank_send_sem, rank_sem.at[k], target
            ).start()
            arrived(passing.at[side], pass_sem.at[side])
            for sy in range(4):
                remote(
                    passing.at[side, sy], members.at[0, pl.ds(t * GROUP + sy * SLOTS, SLOTS)], pass_send_sem,
                    member_sem.at[k], target,
                ).start()

    @pl.when(holds)
    def _():
        best[...] = jnp.full(best.shape, -1.0, jnp.float32)
        sibling = place(x, y, z, 1 - core)

        def scores(side, j0, j1, i0, i1):
            if j0 == j1 or i0 == i1:
                return
            js, iss = pl.ds(j0 * GROUP, (j1 - j0) * GROUP), pl.ds(i0 * GROUP, (i1 - i0) * GROUP)
            found = lax.dot_general(
                members[side, js], members[0, iss], contract_last, preferred_element_type=jnp.float32
            )
            column = jnp.concatenate([rank_column[side, js]] * (i1 - i0), axis=1)
            found = jnp.where(column < rank_row[:, iss], found, -1.0)
            found = jnp.max(found.reshape((j1 - j0) * GROUP // 8, 8, (i1 - i0) * GROUP), axis=0)
            best[:, iss] = jnp.maximum(best[:, iss], found)

        def ranks(side, t0, t1):
            for t in range(t0, t1):
                row = jnp.sum(member_rank[side, t].reshape(4, GROUP), axis=0, keepdims=True)
                if side == 0:
                    rank_row[:, pl.ds(t * GROUP, GROUP)] = row
                rank_column[side, pl.ds(t * GROUP, GROUP)] = jnp.broadcast_to(row, (GROUP, GROUP)).T

        def part(ref, k, side):
            if ref is member_rank:
                return ref.at[side, pl.ds(STARTS[k], STEPS[k])]
            return ref.at[side, pl.ds(STARTS[k] * GROUP, STEPS[k] * GROUP)]

        last = len(STEPS)
        for k in range(last + 1):
            if k < last:
                arrived(part(member_rank, k, 0), rank_sem.at[k])
                remote(
                    part(member_rank, k, 0), part(member_rank, k, 1), pair_rank_send_sem, pair_rank_sem.at[k],
                    sibling,
                ).start()
                arrived(part(members, k, 0), member_sem.at[k])
                remote(
                    part(members, k, 0), part(members, k, 1), pair_send_sem, pair_sem.at[k], sibling
                ).start()
                s, e = STARTS[k], STARTS[k + 1]
                ranks(0, s, e)
                scores(0, s, e, 0, s)
                scores(0, 0, e, s, e)
            else:
                s, e = GROUPS, GROUPS
            if k > 0:
                p, q = STARTS[k - 1], STARTS[k]
                scores(1, 0, p, s, e)
                arrived(part(member_rank, k - 1, 1), pair_rank_sem.at[k - 1])
                arrived(part(members, k - 1, 1), pair_sem.at[k - 1])
                ranks(1, p, q)
                scores(1, p, q, 0, e)

        for t, (dx, dz) in enumerate(ORDER):
            mine_here = best.at[:, pl.ds(t * GROUP, GROUP)]
            for sy in range(4):
                target = place((x + dx) % 4, sy, (z + dz) % 4, core)

                def away():
                    remote(mine_here, back.at[own], back_send_sem, back_sem, target).start()

                if (dx, dz) == (0, 0):
                    pl.when(sy != y)(away)

                    @pl.when(sy == y)
                    def _():
                        pltpu.make_async_copy(mine_here, back.at[own], back_sem).start()
                else:
                    away()

    arrived(back, back_sem)
    table = jnp.max(back[...], axis=1)
    found = lax.dot_general(
        table, onehot, (((0,), (0,)), ((), ())),
        precision=lax.Precision.HIGHEST, preferred_element_type=jnp.float32,
    )
    out_ref[...] = jnp.sum(jnp.where(lane_hit, found, 0.0), axis=0, keepdims=True)

    @pl.when(holds)
    def _():
        arrived(outgoing.at[pl.ds(0, CLUSTERS - 1)], send_sem)
        arrived(out_rank.at[pl.ds(0, CLUSTERS - 1)], rank_send_sem)
        arrived(members.at[0], pair_send_sem)
        arrived(member_rank.at[0], pair_rank_send_sem)
        arrived(back, back_send_sem)
        arrived(back.at[pl.ds(0, CLUSTERS - 1)], back_send_sem)

    @pl.when(jnp.logical_not(holds))
    def _():
        arrived(outgoing, send_sem)
        arrived(out_rank, rank_send_sem)
        arrived(passing, pass_send_sem)
        arrived(passing_rank, pass_rank_send_sem)


def body(embedding, cluster, rank):
    rows, width = embedding.shape
    vmem = pl.BlockSpec(memory_space=pltpu.VMEM)
    dma = pltpu.SemaphoreType.DMA
    steps = len(STEPS)
    found = pl.pallas_call(
        kernel,
        out_shape=jax.ShapeDtypeStruct((1, rows), jnp.float32),
        in_specs=[vmem] * 3,
        out_specs=vmem,
        scratch_shapes=[
            pltpu.VMEM((CLUSTERS, SLOTS, width), jnp.bfloat16),
            pltpu.VMEM((CLUSTERS, 1, GROUP), jnp.float32),
            pltpu.VMEM((2, 4, SLOTS, width), jnp.bfloat16),
            pltpu.VMEM((2, 4, 1, GROUP), jnp.float32),
            pltpu.VMEM((2, GROUPS * GROUP, width), jnp.bfloat16),
            pltpu.VMEM((2, GROUPS, 4, 1, GROUP), jnp.float32),
            pltpu.VMEM((2, GROUPS * GROUP, GROUP), jnp.float32),
            pltpu.VMEM((1, GROUPS * GROUP), jnp.float32),
            pltpu.VMEM((8, GROUPS * GROUP), jnp.float32),
            pltpu.VMEM((CLUSTERS, 8, GROUP), jnp.float32),
            dma, dma, dma((2,)), dma((2,)), dma, dma, dma((steps,)), dma((steps,)),
            dma, dma, dma((steps,)), dma((steps,)), dma, dma,
        ],
        compiler_params=pltpu.CompilerParams(
            collective_id=0, has_side_effects=True, vmem_limit_bytes=56 << 20
        ),
    )(embedding, cluster.reshape(1, rows), rank.reshape(1, rows))
    return found.reshape(rows)


def solution(mesh):
    return jax.shard_map(
        body,
        mesh=mesh,
        in_specs=(P(("shard", "split"), None), P(("shard", "split")), P(("shard", "split"))),
        out_specs=P(("shard", "split")),
        check_vma=False,
    )
```

time: 81.8 us -> 56.8 us (0.69)
  Pallas kernels: 78.6 us -> 55.4 us
  local copies, waits for them, and re-layouts: 2.98 us -> 1.26 us
    pallas_call x1, Pallas kernels: 78.6 us -> 55.4 us  [body(): pl.pallas_call(kernel, out_shape=jax.ShapeDtypeStruct((1, rows), jnp.floa...]
    unnamed x7 -> x1, local copies, waits for them, and re-layouts: 2.98 us -> 1.26 us
where the time goes in v2:
time: 56.8 us; the launch traced here: 56.6 us
  Pallas kernels  55.4 us (98%)
  local copies, waits for them, and re-layouts  1.26 us (2%)
    pallas_call x1, Pallas kernels, body(): pl.pallas_call(kernel, out_shape=jax.ShapeDtypeStruct((1, rows), jnp.floa...  55.4 us
    unnamed x1, local copies, waits for them, and re-layouts  1.26 us

profile of v2, /device:TPU:1, one launch (start us, length us, event | category | flops | bytes accessed | tf_op | source)
XLA Modules:
  0.0 56.6 jit_solution(17709710764852319416)
XLA Ops:
  0.0 55.4 %shard_map.37 = f32[1,512]{1,0:T(1,128)} custom-call(bf16[512,512]{1,0:T(8,128)(2,1)} %embedding_ref.1, s32[1,512]{1,0:T(1,128)} %bitcast.4, s32[1,512]{1,0:T(1,128)} %bitcast.5), custom_call_target="tpu_custom_call" | custom-call | tf_op jit(solution)/shard_map/pallas_call | solution.py:269
  55.4 1.3 %copy.5 = f32[512]{0:T(512)} copy(f32[512]{0:T(512)} %bitcast.3) | data formatting | bytes 4096

commit v3 on v2

--- a/solution.py
+++ b/solution.py
@@ -10,19 +10,24 @@
 SLOTS = 32
 GROUP = 4 * SLOTS
 GROUPS = 16
-PARITY = 1
+PARITY = 0
 NO_RANK = float(1 << 30)
 ORDER = [
-    (1, 2), (3, 2), (2, 2), (0, 2), (2, 1), (2, 3), (1, 1), (3, 3),
-    (3, 1), (1, 3), (0, 1), (0, 3), (2, 0), (1, 0), (3, 0), (0, 0),
+    (0, 0), (1, 0), (3, 0), (2, 0), (0, 1), (1, 1), (3, 1), (2, 1),
+    (0, 3), (3, 3), (0, 2), (1, 2), (3, 2), (1, 3), (2, 2), (2, 3),
 ]
-RELAYED = [(1, 2), (3, 2)]
-STEPS = [4, 4, 4, 2, 1, 1]
+RELAYED = {(1, 3): 1, (2, 2): 3, (2, 3): 1}
+SENDS = list(RELAYED) + [d for d in ORDER[::-1] if d not in RELAYED]
+STEPS = [4, 4, 4, 2, 2]
 STARTS = [sum(STEPS[:k]) for k in range(len(STEPS) + 1)]
 
 
 def place(x, y, z, core):
     return (2 * x + core, 4 * z + y)
+
+
+def turned(dz, odd):
+    return dz if dz % 2 == 0 else (dz + 2 * odd) % 4
 
 
 def step_of(t):
@@ -40,9 +45,9 @@
 
 
 def kernel(
-    embedding_ref, cluster_ref, rank_ref, out_ref,
-    outgoing, out_rank, passing, passing_rank, members, member_rank, rank_column, rank_row, best, back,
-    send_sem, rank_send_sem, pass_sem, pass_rank_sem, pass_send_sem, pass_rank_send_sem, member_sem, rank_sem,
+    embedding_any, cluster_any, rank_any, out_ref,
+    embedding_ref, cluster_ref, rank_ref, outgoing, out_rank, passing, members, member_rank, rank_column, rank_row, best, reply, back,
+    load_sem, send_sem, rank_send_sem, pass_sem, pass_send_sem, member_sem, rank_sem,
     pair_send_sem, pair_rank_send_sem, pair_sem, pair_rank_sem, back_send_sem, back_sem,
 ):
     shard, split = lax.axis_index("shard"), lax.axis_index("split")
@@ -50,6 +55,14 @@
     holds = (x + y + z) % 2 == PARITY
     own = x + 4 * y + 16 * (z // 2)
     rows = embedding_ref.shape[0]
+    loads = [
+        pltpu.make_async_copy(src, dst, load_sem.at[n])
+        for n, (src, dst) in enumerate(
+            [(embedding_any, embedding_ref), (cluster_any, cluster_ref), (rank_any, rank_ref)]
+        )
+    ]
+    for load in loads:
+        load.start()
 
     barrier = pltpu.get_barrier_semaphore()
 
@@ -67,9 +80,12 @@
 
     @pl.when(jnp.logical_not(holds))
     def _():
-        for sy in range(4):
-            greet(x, sy, (z + 2) % 4, core)
-
+        for (dx, dz), aside in RELAYED.items():
+            for sy in range(4):
+                greet((x + 4 - aside + dx) % 4, sy, (z + turned(dz, z % 2)) % 4, core)
+
+    for load in loads:
+        load.wait()
     values = embedding_ref[...].astype(jnp.float32)
     unit = (
         values * lax.rsqrt(jnp.sum(values * values, axis=1, keepdims=True) + 1e-06)
@@ -112,29 +128,44 @@
     mine = lax.broadcasted_iota(jnp.int32, (CLUSTERS, GROUP), 1) // SLOTS == y
     out_rank[...] = jnp.where(mine, jnp.where(taken > 0.5, slot_rank, NO_RANK), 0.0).reshape(CLUSTERS, 1, GROUP)
 
-    pl.semaphore_wait(barrier, CLUSTERS + 2 + jnp.where(holds, 1, 0))
-
-    for t, (dx, dz) in enumerate(ORDER):
-        ax, az = (x + 4 - dx) % 4, (z + 4 - dz) % 4
+    pl.semaphore_wait(barrier, CLUSTERS + 2 * len(RELAYED) + jnp.where(holds, 1, 0))
+
+    for dx, dz in SENDS:
+        ax, az = (x + 4 - dx) % 4, (z + 4 - turned(dz, (z + dz) % 2)) % 4
+        for half in range(2):
+            ay = (y + (ax + y + az + PARITY) % 2 + 2 * half) % 4
+            c = ax + 4 * ay + 16 * (az // 2)
+            there = member_rank.at[0, ORDER.index((dx, dz)), y]
+
+            def away():
+                remote(out_rank.at[c], there, rank_send_sem, rank_sem, place(ax, ay, az, core)).start()
+
+            if (dx, dz) == (0, 0):
+                pl.when(ay != y)(away)
+
+                @pl.when(ay == y)
+                def _():
+                    pltpu.make_async_copy(out_rank.at[c], there, rank_sem).start()
+            else:
+                away()
+
+    for dx, dz in SENDS:
+        t = ORDER.index((dx, dz))
+        ax, az = (x + 4 - dx) % 4, (z + 4 - turned(dz, (z + dz) % 2)) % 4
         for half in range(2):
             ay = (y + (ax + y + az + PARITY) % 2 + 2 * half) % 4
             c = ax + 4 * ay + 16 * (az // 2)
             if (dx, dz) in RELAYED:
-                side = RELAYED.index((dx, dz))
-                target = place(x, ay, az, core)
-                remote(
-                    out_rank.at[c], passing_rank.at[side, y], rank_send_sem, pass_rank_sem.at[side], target
-                ).start()
-                remote(outgoing.at[c], passing.at[side, y], send_sem, pass_sem.at[side], target).start()
+                side = list(RELAYED).index((dx, dz))
+                target = place((ax + RELAYED[dx, dz]) % 4, ay, az, core)
+                remote(outgoing.at[c], passing.at[side, y], send_sem, pass_sem.at[side, y], target).start()
                 continue
             k = step_of(t)
-            rank_there, rank_there_sem = member_rank.at[0, t, y], rank_sem.at[k]
             there = members.at[0, pl.ds(pl.multiple_of(t * GROUP + y * SLOTS, SLOTS), SLOTS)]
             there_sem = member_sem.at[k]
             target = place(ax, ay, az, core)
 
             def away():
-                remote(out_rank.at[c], rank_there, rank_send_sem, rank_there_sem, target).start()
                 remote(outgoing.at[c], there, send_sem, there_sem, target).start()
 
             if (dx, dz) == (0, 0):
@@ -142,26 +173,20 @@
 
                 @pl.when(ay == y)
                 def _():
-                    pltpu.make_async_copy(out_rank.at[c], rank_there, rank_there_sem).start()
                     pltpu.make_async_copy(outgoing.at[c], there, there_sem).start()
             else:
                 away()
 
     @pl.when(jnp.logical_not(holds))
     def _():
-        for side, (dx, dz) in enumerate(RELAYED):
+        for side, ((dx, dz), aside) in enumerate(RELAYED.items()):
             t = ORDER.index((dx, dz))
-            k = step_of(t)
-            target = place((x + 4 - dx) % 4, y, z, core)
-            arrived(passing_rank.at[side], pass_rank_sem.at[side])
-            remote(
-                passing_rank.at[side], member_rank.at[0, t], pass_rank_send_sem, rank_sem.at[k], target
-            ).start()
-            arrived(passing.at[side], pass_sem.at[side])
+            target = place((x + 4 - aside) % 4, y, z, core)
             for sy in range(4):
+                arrived(passing.at[side, sy], pass_sem.at[side, sy])
                 remote(
                     passing.at[side, sy], members.at[0, pl.ds(t * GROUP + sy * SLOTS, SLOTS)], pass_send_sem,
-                    member_sem.at[k], target,
+                    member_sem.at[step_of(t)], target,
                 ).start()
 
     @pl.when(holds)
@@ -181,32 +206,28 @@
             found = jnp.max(found.reshape((j1 - j0) * GROUP // 8, 8, (i1 - i0) * GROUP), axis=0)
             best[:, iss] = jnp.maximum(best[:, iss], found)
 
-        def ranks(side, t0, t1):
-            for t in range(t0, t1):
+        def ranks(side):
+            for t in range(GROUPS):
                 row = jnp.sum(member_rank[side, t].reshape(4, GROUP), axis=0, keepdims=True)
                 if side == 0:
                     rank_row[:, pl.ds(t * GROUP, GROUP)] = row
                 rank_column[side, pl.ds(t * GROUP, GROUP)] = jnp.broadcast_to(row, (GROUP, GROUP)).T
 
-        def part(ref, k, side):
-            if ref is member_rank:
-                return ref.at[side, pl.ds(STARTS[k], STEPS[k])]
-            return ref.at[side, pl.ds(STARTS[k] * GROUP, STEPS[k] * GROUP)]
+        def part(k, side):
+            return members.at[side, pl.ds(STARTS[k] * GROUP, STEPS[k] * GROUP)]
+
+        arrived(member_rank.at[0], rank_sem)
+        remote(member_rank.at[0], member_rank.at[1], pair_rank_send_sem, pair_rank_sem, sibling).start()
+        ranks(0)
+        arrived(member_rank.at[1], pair_rank_sem)
+        ranks(1)
 
         last = len(STEPS)
         for k in range(last + 1):
             if k < last:
-                arrived(part(member_rank, k, 0), rank_sem.at[k])
-                remote(
-                    part(member_rank, k, 0), part(member_rank, k, 1), pair_rank_send_sem, pair_rank_sem.at[k],
-                    sibling,
-                ).start()
-                arrived(part(members, k, 0), member_sem.at[k])
-                remote(
-                    part(members, k, 0), part(members, k, 1), pair_send_sem, pair_sem.at[k], sibling
-                ).start()
+                arrived(part(k, 0), member_sem.at[k])
+                remote(part(k, 0), part(k, 1), pair_send_sem, pair_sem.at[k], sibling).start()
                 s, e = STARTS[k], STARTS[k + 1]
-                ranks(0, s, e)
                 scores(0, s, e, 0, s)
                 scores(0, 0, e, s, e)
             else:
@@ -214,30 +235,28 @@
             if k > 0:
                 p, q = STARTS[k - 1], STARTS[k]
                 scores(1, 0, p, s, e)
-                arrived(part(member_rank, k - 1, 1), pair_rank_sem.at[k - 1])
-                arrived(part(members, k - 1, 1), pair_sem.at[k - 1])
-                ranks(1, p, q)
+                arrived(part(k - 1, 1), pair_sem.at[k - 1])
                 scores(1, p, q, 0, e)
 
         for t, (dx, dz) in enumerate(ORDER):
-            mine_here = best.at[:, pl.ds(t * GROUP, GROUP)]
+            reply[t] = jnp.max(best[:, pl.ds(t * GROUP, GROUP)], axis=0, keepdims=True)
             for sy in range(4):
-                target = place((x + dx) % 4, sy, (z + dz) % 4, core)
+                target = place((x + dx) % 4, sy, (z + turned(dz, z % 2)) % 4, core)
 
                 def away():
-                    remote(mine_here, back.at[own], back_send_sem, back_sem, target).start()
+                    remote(reply.at[t], back.at[own], back_send_sem, back_sem, target).start()
 
                 if (dx, dz) == (0, 0):
                     pl.when(sy != y)(away)
 
                     @pl.when(sy == y)
                     def _():
-                        pltpu.make_async_copy(mine_here, back.at[own], back_sem).start()
+                        pltpu.make_async_copy(reply.at[t], back.at[own], back_sem).start()
                 else:
                     away()
 
     arrived(back, back_sem)
-    table = jnp.max(back[...], axis=1)
+    table = back[...].reshape(CLUSTERS, GROUP)
     found = lax.dot_general(
         table, onehot, (((0,), (0,)), ((), ())),
         precision=lax.Precision.HIGHEST, preferred_element_type=jnp.float32,
@@ -258,7 +277,6 @@
         arrived(outgoing, send_sem)
         arrived(out_rank, rank_send_sem)
         arrived(passing, pass_send_sem)
-        arrived(passing_rank, pass_rank_send_sem)
 
 
 def body(embedding, cluster, rank):
@@ -269,21 +287,24 @@
     found = pl.pallas_call(
         kernel,
         out_shape=jax.ShapeDtypeStruct((1, rows), jnp.float32),
-        in_specs=[vmem] * 3,
+        in_specs=[pl.BlockSpec(memory_space=pl.ANY)] * 3,
         out_specs=vmem,
         scratch_shapes=[
+            pltpu.VMEM((rows, width), jnp.bfloat16),
+            pltpu.VMEM((1, rows), jnp.int32),
+            pltpu.VMEM((1, rows), jnp.int32),
             pltpu.VMEM((CLUSTERS, SLOTS, width), jnp.bfloat16),
             pltpu.VMEM((CLUSTERS, 1, GROUP), jnp.float32),
-            pltpu.VMEM((2, 4, SLOTS, width), jnp.bfloat16),
-            pltpu.VMEM((2, 4, 1, GROUP), jnp.float32),
+            pltpu.VMEM((len(RELAYED), 4, SLOTS, width), jnp.bfloat16),
             pltpu.VMEM((2, GROUPS * GROUP, width), jnp.bfloat16),
             pltpu.VMEM((2, GROUPS, 4, 1, GROUP), jnp.float32),
             pltpu.VMEM((2, GROUPS * GROUP, GROUP), jnp.float32),
             pltpu.VMEM((1, GROUPS * GROUP), jnp.float32),
             pltpu.VMEM((8, GROUPS * GROUP), jnp.float32),
-            pltpu.VMEM((CLUSTERS, 8, GROUP), jnp.float32),
-            dma, dma, dma((2,)), dma((2,)), dma, dma, dma((steps,)), dma((steps,)),
-            dma, dma, dma((steps,)), dma((steps,)), dma, dma,
+            pltpu.VMEM((GROUPS, 1, GROUP), jnp.float32),
+            pltpu.VMEM((CLUSTERS, 1, GROUP), jnp.float32),
+            dma((3,)), dma, dma, dma((len(RELAYED), 4)), dma, dma((steps,)), dma,
+            dma, dma, dma((steps,)), dma, dma, dma,
         ],
         compiler_params=pltpu.CompilerParams(
             collective_id=0, has_side_effects=True, vmem_limit_bytes=56 << 20

time: 56.8 us -> 46 us (0.81)
  Pallas kernels: 55.4 us -> 44.6 us
    pallas_call x1, Pallas kernels: 55.4 us -> 44.6 us  [body(): pl.pallas_call(kernel, out_shape=jax.ShapeDtypeStruct((1, rows), jnp.floa...]
where the time goes in v3:
time: 46 us; the launch traced here: 45.9 us
  Pallas kernels  44.6 us (97%)
  local copies, waits for them, and re-layouts  1.26 us (3%)
    pallas_call x1, Pallas kernels, body(): pl.pallas_call(kernel, out_shape=jax.ShapeDtypeStruct((1, rows), jnp.floa...  44.6 us
    unnamed x1, local copies, waits for them, and re-layouts  1.26 us

profile of v3, /device:TPU:1, one launch (start us, length us, event | category | flops | bytes accessed | tf_op | source)
XLA Modules:
  0.0 45.9 jit_solution(8669396703034109851)
XLA Ops:
  0.0 44.6 %shard_map.37 = f32[1,512]{1,0:T(1,128)} custom-call(bf16[512,512]{1,0:T(8,128)(2,1)} %embedding_any.1, s32[1,512]{1,0:T(1,128)} %bitcast.4, s32[1,512]{1,0:T(1,128)} %bitcast.5), custom_call_target="tpu_custom_call" | custom-call | tf_op jit(solution)/shard_map/pallas_call | solution.py:287
  44.6 1.3 %copy.5 = f32[512]{0:T(512)} copy(f32[512]{0:T(512)} %bitcast.3) | data formatting | bytes 4096

commit v4 on v3

--- a/solution.py
+++ b/solution.py
@@ -14,11 +14,11 @@
 NO_RANK = float(1 << 30)
 ORDER = [
     (0, 0), (1, 0), (3, 0), (2, 0), (0, 1), (1, 1), (3, 1), (2, 1),
-    (0, 3), (3, 3), (0, 2), (1, 2), (3, 2), (1, 3), (2, 2), (2, 3),
+    (1, 3), (3, 3), (0, 2), (1, 2), (3, 2), (2, 3), (2, 2), (0, 3),
 ]
-RELAYED = {(1, 3): 1, (2, 2): 3, (2, 3): 1}
+RELAYED = {(2, 3): 3, (2, 2): 1, (0, 3): 3}
 SENDS = list(RELAYED) + [d for d in ORDER[::-1] if d not in RELAYED]
-STEPS = [4, 4, 4, 2, 2]
+STEPS = [8, 4, 4]
 STARTS = [sum(STEPS[:k]) for k in range(len(STEPS) + 1)]
 
 
@@ -46,7 +46,7 @@
 
 def kernel(
     embedding_any, cluster_any, rank_any, out_ref,
-    embedding_ref, cluster_ref, rank_ref, outgoing, out_rank, passing, members, member_rank, rank_column, rank_row, best, reply, back,
+    embedding_ref, cluster_ref, rank_ref, outgoing, out_rank, passing, members, member_rank, rank_column, rank_row, best, turned_best, reply, back,
     load_sem, send_sem, rank_send_sem, pass_sem, pass_send_sem, member_sem, rank_sem,
     pair_send_sem, pair_rank_send_sem, pair_sem, pair_rank_sem, back_send_sem, back_sem,
 ):
@@ -192,6 +192,7 @@
     @pl.when(holds)
     def _():
         best[...] = jnp.full(best.shape, -1.0, jnp.float32)
+        turned_best[...] = jnp.full(turned_best.shape, -1.0, jnp.float32)
         sibling = place(x, y, z, 1 - core)
 
         def scores(side, j0, j1, i0, i1):
@@ -206,6 +207,25 @@
             found = jnp.max(found.reshape((j1 - j0) * GROUP // 8, 8, (i1 - i0) * GROUP), axis=0)
             best[:, iss] = jnp.maximum(best[:, iss], found)
 
+        def both(j0, j1, i0, i1):
+            if j0 == j1 or i0 == i1:
+                return
+            js, iss = pl.ds(j0 * GROUP, (j1 - j0) * GROUP), pl.ds(i0 * GROUP, (i1 - i0) * GROUP)
+            found = lax.dot_general(
+                members[0, js], members[0, iss], contract_last, preferred_element_type=jnp.float32
+            )
+            column = jnp.concatenate([rank_column[0, js]] * (i1 - i0), axis=1)
+            row = rank_row[:, iss]
+            down = jnp.max(
+                jnp.where(column < row, found, -1.0).reshape((j1 - j0) * GROUP // 8, 8, (i1 - i0) * GROUP), axis=0
+            )
+            best[:, iss] = jnp.maximum(best[:, iss], down)
+            across = jnp.where(row < column, found, -1.0)
+            parts = [across[:, GROUP * n : GROUP * (n + 1)] for n in range(i1 - i0)]
+            while len(parts) > 1:
+                parts = [jnp.maximum(a, b) for a, b in zip(parts[::2], parts[1::2])] + parts[len(parts) // 2 * 2 :]
+            turned_best[js] = jnp.maximum(turned_best[js], parts[0])
+
         def ranks(side):
             for t in range(GROUPS):
                 row = jnp.sum(member_rank[side, t].reshape(4, GROUP), axis=0, keepdims=True)
@@ -224,19 +244,23 @@
 
         last = len(STEPS)
         for k in range(last + 1):
+            s, e = (STARTS[k], STARTS[k + 1]) if k < last else (GROUPS, GROUPS)
             if k < last:
                 arrived(part(k, 0), member_sem.at[k])
                 remote(part(k, 0), part(k, 1), pair_send_sem, pair_sem.at[k], sibling).start()
-                s, e = STARTS[k], STARTS[k + 1]
-                scores(0, s, e, 0, s)
-                scores(0, 0, e, s, e)
-            else:
-                s, e = GROUPS, GROUPS
             if k > 0:
                 p, q = STARTS[k - 1], STARTS[k]
-                scores(1, 0, p, s, e)
                 arrived(part(k - 1, 1), pair_sem.at[k - 1])
                 scores(1, p, q, 0, e)
+                scores(1, 0, p, s, e)
+                if k == last:
+                    for t in range(p):
+                        lanes = pl.ds(t * GROUP, GROUP)
+                        other = jnp.max(turned_best[lanes].T.reshape(GROUP // 8, 8, GROUP), axis=0)
+                        best[:, lanes] = jnp.maximum(best[:, lanes], other)
+            if k < last:
+                both(0, s, s, e)
+                scores(0, s, e, s, e)
 
         for t, (dx, dz) in enumerate(ORDER):
             reply[t] = jnp.max(best[:, pl.ds(t * GROUP, GROUP)], axis=0, keepdims=True)
@@ -301,6 +325,7 @@
             pltpu.VMEM((2, GROUPS * GROUP, GROUP), jnp.float32),
             pltpu.VMEM((1, GROUPS * GROUP), jnp.float32),
             pltpu.VMEM((8, GROUPS * GROUP), jnp.float32),
+            pltpu.VMEM((STARTS[-2] * GROUP, GROUP), jnp.float32),
             pltpu.VMEM((GROUPS, 1, GROUP), jnp.float32),
             pltpu.VMEM((CLUSTERS, 1, GROUP), jnp.float32),
             dma((3,)), dma, dma, dma((len(RELAYED), 4)), dma, dma((steps,)), dma,

time: 46 us -> 44.4 us (0.965)
  Pallas kernels: 44.6 us -> 42.7 us
    pallas_call x1, Pallas kernels: 44.6 us -> 42.7 us  [body(): pl.pallas_call(kernel, out_shape=jax.ShapeDtypeStruct((1, rows), jnp.floa...]
where the time goes in v4:
time: 44.4 us; the launch traced here: 44 us
  Pallas kernels  42.7 us (96%)
  local copies, waits for them, and re-layouts  1.26 us (3%)
    pallas_call x1, Pallas kernels, body(): pl.pallas_call(kernel, out_shape=jax.ShapeDtypeStruct((1, rows), jnp.floa...  42.7 us
    unnamed x1, local copies, waits for them, and re-layouts  1.26 us

profile of v4, /device:TPU:1, one launch (start us, length us, event | category | flops | bytes accessed | tf_op | source)
XLA Modules:
  0.0 44.0 jit_solution(9399192787792133318)
XLA Ops:
  0.0 42.7 %shard_map.37 = f32[1,512]{1,0:T(1,128)} custom-call(bf16[512,512]{1,0:T(8,128)(2,1)} %embedding_any.1, s32[1,512]{1,0:T(1,128)} %bitcast.4, s32[1,512]{1,0:T(1,128)} %bitcast.5), custom_call_target="tpu_custom_call" | custom-call | tf_op jit(solution)/shard_map/pallas_call | solution.py:311
  42.7 1.3 %copy.5 = f32[512]{0:T(512)} copy(f32[512]{0:T(512)} %bitcast.3) | data formatting | bytes 4096

commit v5 on v4

--- a/solution.py
+++ b/solution.py
@@ -71,11 +71,8 @@
 
     @pl.when(holds)
     def _():
-        def each(s, carry):
-            greet(s % 4, (s // 4) % 4, s // 16, core)
-            return carry
-
-        lax.fori_loop(0, 64, each, 0)
+        for s in range(64):
+            greet(s % 4, s // 4 % 4, s // 16, core)
         greet(x, y, z, 1 - core)
 
     @pl.when(jnp.logical_not(holds))
@@ -101,15 +98,12 @@
     position = jnp.sum(before * onehot, axis=0, keepdims=True).astype(jnp.int32)
     slot = cluster * SLOTS + position
 
-    def fill(part, carry):
+    for part in range(CLUSTERS * SLOTS // 256):
         pick = (
             lax.broadcasted_iota(jnp.int32, (256, rows), 0) + part * 256 == slot
         ).astype(jnp.float32).astype(jnp.bfloat16)
         packed = jnp.dot(pick, unit, preferred_element_type=jnp.float32).astype(jnp.bfloat16)
         outgoing[pl.ds(part * 8, 8)] = packed.reshape(8, SLOTS, packed.shape[1])
-        return carry
-
-    lax.fori_loop(0, CLUSTERS * SLOTS // 256, fill, 0)
 
     lane_hit = lax.broadcasted_iota(jnp.int32, (GROUP, rows), 0) == position + SLOTS * y
     lane_onehot = lane_hit.astype(jnp.float32).astype(jnp.bfloat16)

time: 44.4 us -> 43.7 us (0.984)
  Pallas kernels: 42.7 us -> 42.2 us
where the time goes in v5:
time: 43.7 us; the launch traced here: 43.5 us
  Pallas kernels  42.2 us (97%)
  local copies, waits for them, and re-layouts  1.26 us (3%)
    pallas_call x1, Pallas kernels, body(): pl.pallas_call(kernel, out_shape=jax.ShapeDtypeStruct((1, rows), jnp.floa...  42.2 us
    unnamed x1, local copies, waits for them, and re-layouts  1.26 us

profile of v5, /device:TPU:1, one launch (start us, length us, event | category | flops | bytes accessed | tf_op | source)
XLA Modules:
  0.0 43.5 jit_solution(1225341612993839506)
XLA Ops:
  0.0 42.2 %shard_map.37 = f32[1,512]{1,0:T(1,128)} custom-call(bf16[512,512]{1,0:T(8,128)(2,1)} %embedding_any.1, s32[1,512]{1,0:T(1,128)} %bitcast.4, s32[1,512]{1,0:T(1,128)} %bitcast.5), custom_call_target="tpu_custom_call" | custom-call | tf_op jit(solution)/shard_map/pallas_call | solution.py:305
  42.3 1.3 %copy.5 = f32[512]{0:T(512)} copy(f32[512]{0:T(512)} %bitcast.3) | data formatting | bytes 4096

commit v6 on v5

--- a/solution.py
+++ b/solution.py
@@ -275,9 +275,13 @@
 
     arrived(back, back_sem)
     table = back[...].reshape(CLUSTERS, GROUP)
+    high = table.astype(jnp.bfloat16)
+    rest = table - high.astype(jnp.float32)
+    middle = rest.astype(jnp.bfloat16)
+    low = (rest - middle.astype(jnp.float32)).astype(jnp.bfloat16)
     found = lax.dot_general(
-        table, onehot, (((0,), (0,)), ((), ())),
-        precision=lax.Precision.HIGHEST, preferred_element_type=jnp.float32,
+        jnp.concatenate([high, middle, low], axis=0), jnp.concatenate([onehot.astype(jnp.bfloat16)] * 3, axis=0),
+        (((0,), (0,)), ((), ())), preferred_element_type=jnp.float32,
     )
     out_ref[...] = jnp.sum(jnp.where(lane_hit, found, 0.0), axis=0, keepdims=True)
 

time: 43.7 us -> 43.5 us (level)
  no operation moved by 1% of the time
where the time goes in v6:
time: 43.5 us; the launch traced here: 43.4 us
  Pallas kernels  42.1 us (97%)
  local copies, waits for them, and re-layouts  1.26 us (3%)
    pallas_call x1, Pallas kernels, body(): pl.pallas_call(kernel, out_shape=jax.ShapeDtypeStruct((1, rows), jnp.floa...  42.1 us
    unnamed x1, local copies, waits for them, and re-layouts  1.26 us

profile of v6, /device:TPU:1, one launch (start us, length us, event | category | flops | bytes accessed | tf_op | source)
XLA Modules:
  0.0 43.4 jit_solution(6205200463691326861)
XLA Ops:
  0.0 42.1 %shard_map.37 = f32[1,512]{1,0:T(1,128)} custom-call(bf16[512,512]{1,0:T(8,128)(2,1)} %embedding_any.1, s32[1,512]{1,0:T(1,128)} %bitcast.4, s32[1,512]{1,0:T(1,128)} %bitcast.5), custom_call_target="tpu_custom_call" | custom-call | tf_op jit(solution)/shard_map/pallas_call | solution.py:309
  42.1 1.3 %copy.5 = f32[512]{0:T(512)} copy(f32[512]{0:T(512)} %bitcast.3) | data formatting | bytes 4096
